TPU v7x, 256 devices: a whole 4x4x8 slice. The times are simulated.
256 devices in a mesh: dp: 16 (over z_hi, y, core), tensor: 16 (over z_lo, x).
Axes of the slice: x: 4, y: 4, z: 8 (z_hi: 2, z_lo: 4; z = z_hi * 4 + z_lo), core: 2. Of those that a mesh axis runs over, the one named last changes fastest.
Arguments:
- hidden: bfloat16 [2048, 26624], P('dp', 'tensor'), parts along dimension 0, may hold values from -6 to 6
- residual: bfloat16 [2048, 8320], P(('dp', 'tensor')), parts along dimension 0, may hold values from -6 to 6
- sign_bits: int32 [26624], P('tensor'), may hold values from 0 to 1
- packed: float32 [26624, 1664], P('tensor'), may hold values from 0 to 1048575, as said below
- scales: float32 [8320], replicated, may hold values from 0.0006 to 0.004
Outputs:
- layer_out: bfloat16 [2048, 8320], P(('dp', 'tensor')), parts along dimension 0
There are 16 independent parts, one for each index of `dp`. A program takes and returns all parts, laid end to end along the dimension named above; an argument that names none is the same for every part. Nothing has to cross between parts.
Inputs may be any that keep to these rules, and one draw needn't show every extreme that they name: `sign_bits`: 0 flips the sign of a hidden unit before the rotation. `packed`: each word is a whole number; its base-16 digit k holds the code plus 8 of output feature 5j+k for hidden unit f, k = 0 to 4.
All inputs are finite; a program needn't handle non-finite values.
Results may differ from a plain program's by a relative error of at most 0.025.
Values may be sent and summed in bfloat16 or wider, within the bound.
A program may use at most 192 MiB of HBM per device.

v0:
```python
import math

import jax
import jax.numpy as jnp
from jax import lax
from jax.sharding import PartitionSpec as P

WALSH = 2048
ODD = 13


def partner_2(value, axis, apart):
    return lax.ppermute(value, axis, [(i, i ^ 1 << apart) for i in range(lax.axis_size(axis))])


def dct_table():
    frequency = jnp.arange(ODD, dtype=jnp.float32)[:, None]
    sample = jnp.arange(ODD, dtype=jnp.float32)[None, :]
    weights = jnp.where(frequency == 0, math.sqrt(0.5), 1.0) * math.sqrt(2.0 / ODD)
    return weights * jnp.cos(math.pi * (2.0 * sample + 1.0) * frequency / (2.0 * ODD))


def walsh_signs(length):
    row_ids = jnp.arange(length, dtype=jnp.int32)[:, None]
    col_ids = jnp.arange(length, dtype=jnp.int32)[None, :]
    parity = jnp.zeros((length, length), jnp.int32)
    for bit_number in range(length.bit_length() - 1):
        row_bit = jnp.bitwise_and(jnp.right_shift(row_ids, bit_number), 1)
        col_bit = jnp.bitwise_and(jnp.right_shift(col_ids, bit_number), 1)
        parity = parity + row_bit * col_bit
    return (1 - 2 * jnp.bitwise_and(parity, 1)).astype(jnp.float32)


def local_turn(rows, local_len):
    row_count = rows.shape[0]
    viewed = rows.reshape(row_count, local_len, ODD)
    walshed = jnp.einsum(
        "tcb,ca->tba", viewed, walsh_signs(local_len), precision=lax.Precision.HIGHEST
    )
    turned = jnp.einsum("tba,kb->tak", walshed, dct_table(), precision=lax.Precision.HIGHEST)
    return (turned / math.sqrt(WALSH)).reshape(row_count, local_len * ODD)


def shards(hidden, residual, sign_bits, packed, scales):
    sign_flips = (2 * sign_bits - 1).astype(jnp.bfloat16)
    flipped = hidden * sign_flips[None, :]
    tokens, row_width = hidden.shape
    groups = lax.axis_size("tensor")
    local_len = row_width // ODD
    mixed_rows = flipped.astype(jnp.float32)
    position = lax.axis_index("tensor")
    for bit_number in range(groups.bit_length() - 1):
        partner = partner_2(mixed_rows.astype(jnp.bfloat16), "tensor", bit_number).astype(
            mixed_rows.dtype
        )
        upper_half = jnp.bitwise_and(jnp.right_shift(position, bit_number), 1) == 1
        mixed_rows = jnp.where(upper_half, partner - mixed_rows, mixed_rows + partner)
    rotated = local_turn(mixed_rows, local_len).astype(jnp.bfloat16)
    digits = [jnp.mod(jnp.floor_divide(packed, 16.0**place), 16.0) - 8.0 for place in range(5)]
    weight_codes = (
        jnp.stack(digits, axis=2).reshape(packed.shape[0], packed.shape[1] * 5).astype(jnp.bfloat16)
    )
    partial_out = (
        jnp.dot(rotated, weight_codes, preferred_element_type=jnp.float32) * scales[None, :]
    )
    summed = lax.psum_scatter(
        partial_out.astype(jnp.bfloat16), "tensor", scatter_dimension=0, tiled=True
    ).astype(jnp.float32)
    return (residual.astype(jnp.float32) + summed).astype(jnp.bfloat16)


def solution(mesh):
    return jax.shard_map(
        shards,
        mesh=mesh,
        in_specs=(
            P("dp", "tensor"),
            P(("dp", "tensor"), None),
            P("tensor"),
            P("tensor", None),
            P(),
        ),
        out_specs=P(("dp", "tensor"), None),
        check_vma=False,
    )
```

profile of v0, /device:TPU:16, one launch (start us, length us, event | category | flops | bytes accessed | tf_op | source)
XLA Modules:
  0.0 423.8 jit_solution(13256114898647042849)
XLA Ops:
  6.5 0.9 add_convert_fusion.1
  7.4 1.2 broadcast_multiply_fusion
  8.6 1.6 collective-permute-start
  10.2 15.0 %bitcast_dynamic-update-slice_fusion.4 = bf16[1664,1664,5]{1,0,2:T(8,128)(2,1)S(1)} fusion(f32[1664,1664]{1,0:T(8,128)} %param.18), kind=kLoop, calls=%fused_computation.65 | loop fusion | flops 47071232 | bytes 16613376
  25.1 15.2 %bitcast_dynamic-update-slice_fusion.3 = bf16[1664,1664,5]{1,0,2:T(8,128)(2,1)S(1)} fusion(bf16[1664,1664,5]{1,0,2:T(8,128)(2,1)S(1)} %bitcast_dynamic-update-slice_fusion.4, f32[1664,1664]{1,0:T(8,128)S(1)} %copy-done), kind=kLoop, calls=%fused_computation.64 | loop fusion | flops 49840128 | bytes 16613376
  40.3 15.2 %bitcast_dynamic-update-slice_fusion.2 = bf16[1664,1664,5]{1,0,2:T(8,128)(2,1)S(1)} fusion(bf16[1664,1664,5]{1,0,2:T(8,128)(2,1)S(1)} %bitcast_dynamic-update-slice_fusion.3, f32[1664,1664]{1,0:T(8,128)S(1)} %copy-done), kind=kLoop, calls=%fused_computation.63 | loop fusion | flops 49840128 | bytes 16613376
  55.5 9.1 %copy-done.1 = bf16[1664,1664,5]{1,0,2:T(8,128)(2,1)} copy-done((bf16[1664,1664,5]{1,0,2:T(8,128)(2,1)}, bf16[1664,1664,5]{1,0,2:T(8,128)(2,1)S(1)}, u32[]{:S(2)}) %copy-start.1) | copy-done | bytes 27688984
  64.8 2.8 collective-permute-start.1
  67.6 16.8 %bitcast_dynamic-update-slice_fusion.1 = bf16[1664,1664,5]{1,0,2:T(8,128)(2,1)} fusion(bf16[1664,1664,5]{1,0,2:T(8,128)(2,1)} %copy-done.1, f32[1664,1664]{1,0:T(8,128)} %param.18), kind=kLoop, calls=%fused_computation.62 | loop fusion | flops 49840128 | bytes 16613376
  84.8 2.0 collective-permute-start.2
  86.8 16.8 %bitcast_dynamic-update-slice_fusion = bf16[1664,1664,5]{1,0,2:T(8,128)(2,1)} fusion(bf16[1664,1664,5]{1,0,2:T(8,128)(2,1)} %bitcast_dynamic-update-slice_fusion.1, f32[1664,1664]{1,0:T(8,128)} %param.18), kind=kLoop, calls=%fused_computation.61 | loop fusion | flops 49840128 | bytes 16613376 | tf_op jit(solution)/shard_map/stack | solution.py:61
  103.6 58.4 %copy.13 = bf16[1664,1664,5]{0,2,1:T(8,128)(2,1)} copy(bf16[1664,1664,5]{1,0,2:T(8,128)(2,1)} %bitcast_dynamic-update-slice_fusion) | data formatting | bytes 55377920 | tf_op jit(solution)/shard_map/stack | solution.py:61
  162.0 44.0 %convert_element_type.72 = bf16[1664,8320]{0,1:T(8,128)(2,1)} reshape(bf16[1664,1664,5]{0,2,1:T(8,128)(2,1)} %copy.13) | data formatting | bytes 55377920 | tf_op jit(solution)/shard_map/convert_element_type | solution.py:61
  206.0 0.4 fusion.44
  206.4 3.5 collective-permute-start.3
  210.0 18.1 %collective-permute-done.3 = bf16[128,1664]{1,0:T(8,128)(2,1)S(1)} collective-permute-done((bf16[128,1664]{1,0:T(8,128)(2,1)S(1)}, bf16[128,1664]{1,0:T(8,128)(2,1)S(1)}, u32[]{:S(2)}, u32[]{:S(2)}) %collective-permute-start.3) | collective-permute-done | bytes 426016 | tf_op jit(solution)/shard_map/ppermute | solution.py:13
  228.0 0.5 fusion.40
  228.9 1.7 fusion.41
  230.6 1.7 fusion.35
  232.3 0.7 copy.12
  233.2 14.5 %fusion.34 = bf16[128,8320]{1,0:T(8,128)(2,1)} fusion(bf16[128,1664]{0,1:T(8,128)(2,1)S(1)} %convert_element_type.71, bf16[1664,8320]{0,1:T(8,128)(2,1)} %convert_element_type.72, f32[8320]{0:T(1024)S(1)} %copy-done.4), kind=kOutput, calls=%fused_computation.60 | convolution fusion | flops 3546316800 | bytes 30278144 | tf_op jit(solution)/shard_map/dot_general | solution.py:64
  247.8 0.6 dynamic-slice
  249.0 166.3 %all-reduce.3.cloned.1.call-done = bf16[128,8320]{1,0:T(8,128)(2,1)} async-done(((bf16[128,8320]{1,0:T(8,128)(2,1)}), bf16[128,8320]{1,0:T(8,128)(2,1)}) %all-reduce.3.cloned.1.call-update) | async-done | bytes 2129936
  415.3 1.6 add_convert_fusion
  (26 shorter events, 1.1 us)
Async XLA Ops:
  6.5 408.8 %all-reduce.3.cloned.1.call-start = ((), (), s32[]{:S(2)}) async-start(), calls=%async_computation | async-start | bytes 4259840
  6.5 18.6 %copy-start = (f32[1664,1664]{1,0:T(8,128)S(1)}, f32[1664,1664]{1,0:T(8,128)}, u32[]{:S(2)}) copy-start(f32[1664,1664]{1,0:T(8,128)} %param.18) | copy-start | bytes 33226756
  8.6 56.1 %collective-permute-start = (bf16[128,1664]{1,0:T(8,128)(2,1)S(1)}, bf16[128,1664]{1,0:T(8,128)(2,1)S(1)}, u32[]{:S(2)}, u32[]{:S(2)}) collective-permute-start(bf16[128,1664]{1,0:T(8,128)(2,1)S(1)} %broadcast_multiply_fusion), channel_id=1, source_target_pairs={{0,1},{1,0},{2,3},{3,2},{4,5},{5,4},{6,7},{7,6},{8,9},{9,8},{10,11... | collective-permute-start | bytes 1277960 | tf_op jit(solution)/shard_map/ppermute | solution.py:13
  40.3 24.3 %copy-start.2 = (bf16[128,1664]{1,0:T(8,128)(2,1)S(1)}, bf16[128,1664]{1,0:T(8,128)(2,1)}, u32[]{:S(2)}) copy-start(bf16[128,1664]{1,0:T(8,128)(2,1)} %param.15) | copy-start | bytes 1277956
  55.5 9.1 %copy-start.1 = (bf16[1664,1664,5]{1,0,2:T(8,128)(2,1)}, bf16[1664,1664,5]{1,0,2:T(8,128)(2,1)S(1)}, u32[]{:S(2)}) copy-start(bf16[1664,1664,5]{1,0,2:T(8,128)(2,1)S(1)} %bitcast_dynamic-update-slice_fusion.2) | copy-start | bytes 83066880
  64.8 19.6 %collective-permute-start.1 = (bf16[128,1664]{1,0:T(8,128)(2,1)S(1)}, bf16[128,1664]{1,0:T(8,128)(2,1)S(1)}, u32[]{:S(2)}, u32[]{:S(2)}) collective-permute-start(bf16[128,1664]{1,0:T(8,128)(2,1)S(1)} %fusion.43), channel_id=1, source_target_pairs={{0,2},{1,3},{2,0},{3,1},{4,6},{5,7},{6,4},{7,5},{8,10},{9,11},{10,... | collective-permute-start | bytes 1277960 | tf_op jit(solution)/shard_map/ppermute | solution.py:13
  84.8 121.2 %collective-permute-start.2 = (bf16[128,1664]{1,0:T(8,128)(2,1)S(1)}, bf16[128,1664]{1,0:T(8,128)(2,1)S(1)}, u32[]{:S(2)}, u32[]{:S(2)}) collective-permute-start(bf16[128,1664]{1,0:T(8,128)(2,1)S(1)} %fusion.92), channel_id=1, source_target_pairs={{0,4},{1,5},{2,6},{3,7},{4,0},{5,1},{6,2},{7,3},{8,12},{9,13},{10,... | collective-permute-start | bytes 1277960 | tf_op jit(solution)/shard_map/ppermute | solution.py:13
  206.0 27.2 %copy-start.4 = (f32[8320]{0:T(1024)S(1)}, f32[8320]{0:T(1024)}, u32[]{:S(2)}) copy-start(f32[8320]{0:T(1024)} %param.19) | copy-start | bytes 99844
  206.4 21.6 %collective-permute-start.3 = (bf16[128,1664]{1,0:T(8,128)(2,1)S(1)}, bf16[128,1664]{1,0:T(8,128)(2,1)S(1)}, u32[]{:S(2)}, u32[]{:S(2)}) collective-permute-start(bf16[128,1664]{1,0:T(8,128)(2,1)S(1)} %fusion.44), channel_id=1, source_target_pairs={{0,8},{1,9},{2,10},{3,11},{4,12},{5,13},{6,14},{7,15},{8,0},{9,1},... | collective-permute-start | bytes 1277960 | tf_op jit(solution)/shard_map/ppermute | solution.py:13
  233.2 14.6 %copy-start.5 = (u32[256]{0:T(256)S(1)}, u32[256]{0:T(256)}, u32[]{:S(2)}) copy-start(u32[256]{0:T(256)} %constant.138) | copy-start | bytes 3076
  233.2 182.1 %copy-start.3 = (bf16[8,8320]{1,0:T(8,128)(2,1)S(1)}, bf16[8,8320]{1,0:T(8,128)(2,1)}, u32[]{:S(2)}) copy-start(bf16[8,8320]{1,0:T(8,128)(2,1)} %param.16) | copy-start | bytes 399364
Sparse Core Ops, SparseCore 0:
  247.9 167.4 all-reduce.2
where the time goes:
time: 427 us; the launch traced here: 424 us
  waiting for transfers between devices  184 us (43%)
  local copies, waits for them, and re-layouts  113 us (26%)
  other arithmetic  84 us (20%)
  matrix products  17.9 us (4%)
  between operations  14.2 us (3%)
  starting transfers between devices  9.94 us (2%)
    unnamed x2, waiting for transfers between devices  166 us
    unnamed x4, other arithmetic  62.1 us
    another operation x1, local copies, waits for them, and re-layouts, shards(): jnp.stack(digits, axis=2).reshape(packed.shape[0], packed.shape[1] * 5)  58.4 us
    convert_element_type x1, local copies, waits for them, and re-layouts, shards(): jnp.stack(digits, axis=2).reshape(packed.shape[0], packed.shape[1] * 5)  44 us
    ppermute x4, waiting for transfers between devices, partner_2(): lax.ppermute(value, axis, [(i, i ^ 1 << apart) for i in range(lax.axis_si...  18.1 us
    another operation x1, other arithmetic, shards(): jnp.stack(digits, axis=2).reshape(packed.shape[0], packed.shape[1] * 5)  16.8 us
    dot_general x1, matrix products, shards(): jnp.dot(rotated, weight_codes, preferred_element_type=jnp.float32)  14.5 us
    ppermute x4, starting transfers between devices, partner_2(): lax.ppermute(value, axis, [(i, i ^ 1 << apart) for i in range(lax.axis_si...  9.94 us
  transfers between devices with their start and end apart: 5, of which 2 were waited for; matrix products, arithmetic and copies ran while one was open for 43% of the time, Pallas kernels for 0%

commit v1 on v0

v1 whole, which is shorter than its diff:
```python
import math

import jax
import jax.numpy as jnp
import numpy as np
from jax import lax
from jax.experimental import pallas as pl
from jax.experimental.pallas import tpu as pltpu
from jax.sharding import PartitionSpec as P

WALSH = 2048
ODD = 13
GROUPS = 16
NX = 4
NZ = 4
TOK = 128
ROW = 1664
DIGITS = 5
LANE = 128
WIDE = 2 * LANE
PAIRS = 7
TILES = 13
BLOCK = DIGITS * LANE
SLOTS = 4
MESH = pl.DeviceIdType.MESH
F32 = jnp.float32
BF16 = jnp.bfloat16


def turn_table():
    local = ROW // ODD
    ids = np.arange(local)
    both = ids[:, None] & ids[None, :]
    parity = np.zeros_like(both)
    for bit in range(local.bit_length() - 1):
        parity ^= (both >> bit) & 1
    walsh = 1.0 - 2.0 * parity
    k = np.arange(ODD)[:, None]
    b = np.arange(ODD)[None, :]
    cosine = np.where(k == 0, math.sqrt(0.5), 1.0) * math.sqrt(2.0 / ODD)
    cosine = cosine * np.cos(math.pi * (2.0 * b + 1.0) * k / (2.0 * ODD))
    return (np.kron(walsh, cosine.T) / math.sqrt(WALSH)).astype(jnp.bfloat16)


def peers(me):
    z, x = me // NX, me % NX
    out = []
    for dz in (2, 1, 3, 0):
        for dx in (2, 1, 3, 0):
            if dz or dx:
                out.append((dz * NX + dx, (z + dz) % NZ * NX + (x + dx) % NX))
    return out


def kernel(
    hid, res, sgn, packed, scl, turn, out,
    hid_v, res_v, sgn_v, scl_v, turn_v, words, codes, perm,
    rx, mixed, tx, rr, lhs, part, in1, out2, in2, summed, in3, fin,
    load_sem, word_sem, s1, r1, s2, r2, sx1, rx1, sx2, rx2, sz, rz,
):
    me = lax.axis_index("tensor")
    z, x = me // NX, me % NX
    loads = []
    for n, (src, dst) in enumerate(
        ((hid, hid_v), (sgn, sgn_v), (turn, turn_v), (res, res_v), (scl, scl_v))
    ):
        loads.append(pltpu.make_async_copy(src, dst, load_sem.at[n]))

    def word_copy(r, slot):
        return pltpu.make_async_copy(
            packed.at[pl.ds(pl.multiple_of(r * LANE, LANE), LANE)], words.at[slot], word_sem.at[slot]
        )

    loads[0].start()
    loads[1].start()
    barrier = pltpu.get_barrier_semaphore()
    for _, peer in peers(me):
        pl.semaphore_signal(barrier, inc=1, device_id={"tensor": peer}, device_id_type=MESH)
    for r in range(SLOTS):
        word_copy(r, r).start()
    for n in (2, 3, 4):
        loads[n].start()

    loads[0].wait()
    loads[1].wait()
    flips = (2 * sgn_v[...] - 1).astype(F32)

    @pl.loop(0, GROUPS)
    def _(g):
        hid_v[g] = (hid_v[g].astype(F32) * flips).astype(BF16)

    pl.semaphore_wait(barrier, GROUPS - 1)

    def send(src, dst, sem_s, sem_r):
        copies = []
        for off, peer in peers(me):
            copy = pltpu.make_async_remote_copy(
                src_ref=src.at[peer], dst_ref=dst.at[me], send_sem=sem_s.at[off], recv_sem=sem_r.at[off],
                device_id={"tensor": peer}, device_id_type=MESH,
            )
            copy.start()
            copies.append(copy)
        return copies

    def unpack(r):
        slot = r % SLOTS
        word_copy(r, slot).wait()
        rows = pl.ds(pl.multiple_of(r * LANE, LANE), LANE)
        for p in range(PAIRS):
            wide = WIDE if p < PAIRS - 1 else LANE
            word = words[slot, :, p * WIDE : p * WIDE + wide].astype(jnp.int32) ^ 0x88888
            for k in range(DIGITS):
                digit = (word << (28 - 4 * k)) >> 28
                codes[p * DIGITS + k, rows, :wide] = digit.astype(F32).astype(BF16)

        @pl.when(r + SLOTS < TILES)
        def _():
            word_copy(r + SLOTS, slot).start()

    sent1 = send(hid_v, rx, s1, r1)
    rx[me] = hid_v[me]
    first_rows = 6

    @pl.loop(0, first_rows)
    def _(r):
        unpack(r)

    rows = lax.broadcasted_iota(jnp.int32, (BLOCK, BLOCK), 0)
    cols = lax.broadcasted_iota(jnp.int32, (BLOCK, BLOCK), 1)
    perm[...] = jnp.where((rows & (LANE - 1)) * DIGITS + (rows >> 7) == cols, 1.0, 0.0).astype(BF16)
    fin[...] = jnp.zeros_like(fin)

    for copy in sent1:
        copy.wait_recv()

    @pl.loop(0, TILES)
    def _(c):
        lanes = pl.ds(pl.multiple_of(c * LANE, LANE), LANE)
        blocks = [rx[g, :, lanes].astype(F32) for g in range(GROUPS)]
        span = 1
        while span < GROUPS:
            for g in range(GROUPS):
                if not g & span:
                    a, b = blocks[g], blocks[g + span]
                    blocks[g], blocks[g + span] = a + b, a - b
            span *= 2
        mixed[:, lanes] = jnp.concatenate(blocks, axis=0).astype(BF16)

    loads[2].wait()

    def turned(start, wide):
        lanes = pl.ds(start, wide)
        y = jnp.dot(mixed[...], turn_v[:, lanes], preferred_element_type=F32)
        tx[:, :, lanes] = y.reshape(GROUPS, TOK // GROUPS, wide).astype(BF16)

    @pl.loop(0, PAIRS - 1)
    def _(c):
        turned(pl.multiple_of(c * WIDE, WIDE), WIDE)

    turned((PAIRS - 1) * WIDE, LANE)
    sent2 = send(tx, rr, s2, r2)
    rr[me] = tx[me]

    @pl.loop(first_rows, TILES)
    def _(r):
        unpack(r)

    loads[3].wait()
    loads[4].wait()
    for copy in sent2:
        copy.wait_recv()

    @pl.loop(0, TILES)
    def _(c):
        lanes = pl.ds(pl.multiple_of(c * LANE, LANE), LANE)
        lhs[:, lanes] = rr[:, :, lanes].astype(F32).reshape(TOK, LANE).astype(BF16)

    across = (x + 1 - 2 * (x % 2), 3 - x)
    half = ((x + 1) // 2 % 2, x // 2)
    mine = (x // 2, x % 2)
    place = ((0, 2, 3, 1), (0, 1, 2, 3))

    def first(p, t):
        return pltpu.make_async_remote_copy(
            src_ref=part.at[p, t, pl.ds(2 * (1 - half[t]), 2)], dst_ref=in1.at[p, t],
            send_sem=sx1.at[p, t], recv_sem=rx1.at[p, t],
            device_id={"tensor": z * NX + across[t]}, device_id_type=MESH,
        )

    def second(p, t):
        return pltpu.make_async_remote_copy(
            src_ref=out2.at[p, t], dst_ref=in2.at[p, t], send_sem=sx2.at[p, t], recv_sem=rx2.at[p, t],
            device_id={"tensor": z * NX + across[1 - t]}, device_id_type=MESH,
        )

    def third(p, dz, tiles):
        there = (z + dz) % NZ
        return pltpu.make_async_remote_copy(
            src_ref=summed.at[p, there, pl.ds(0, tiles)], dst_ref=in3.at[p, dz - 1, pl.ds(0, tiles)],
            send_sem=sz.at[p, dz - 1], recv_sem=rz.at[p, dz - 1],
            device_id={"tensor": there * NX + x}, device_id_type=MESH,
        )

    def multiply(p, tiles):
        for k in range(DIGITS):
            y = jnp.dot(lhs[...], codes[p * DIGITS + k, :, : tiles * LANE], preferred_element_type=F32)
            y = y.reshape(NZ, NX, TOK // GROUPS, tiles * LANE)
            for t in range(tiles):
                for xx in range(NX):
                    part[p, t, place[t][xx], :, :, k * LANE : (k + 1) * LANE] = y[
                        :, xx, :, t * LANE : (t + 1) * LANE
                    ].astype(BF16)
        for t in range(tiles):
            first(p, t).start()

    def halve(p, tiles):
        for t in range(tiles):
            first(p, t).wait_recv()
            other = 1 - mine[t]
            out2[p, t] = (
                part[p, t, 2 * half[t] + other].astype(F32) + in1[p, t, other].astype(F32)
            ).astype(BF16)
            second(p, t).start()

    def spread(p, tiles):
        for t in range(tiles):
            second(p, t).wait_recv()
            total = part[p, t, 2 * half[t] + mine[t]].astype(F32) + in1[p, t, mine[t]].astype(F32)
            summed[p, :, t] = (total + in2[p, t].astype(F32)).astype(BF16)
        for dz in (2, 1, 3):
            third(p, dz, tiles).start()

    def gather(p, tiles):
        for dz in (2, 1, 3):
            third(p, dz, tiles).wait_recv()
        total = summed[p, z, :tiles].astype(F32)
        for n in range(NZ - 1):
            total = total + in3[p, n, :tiles].astype(F32)
        total = total.reshape(tiles * 8, BLOCK)
        if tiles == 1:
            total = jnp.concatenate([total, jnp.zeros_like(total)], axis=0)
        high = total.astype(BF16)
        rows = pl.ds(pl.multiple_of(p * 16, 16), 16)
        fin[0, rows, :] = high
        fin[1, rows, :] = (total - high.astype(F32)).astype(BF16)

    stages = (multiply, halve, spread, gather)
    lags = (0, 1, 2, 3)
    last = PAIRS - 1
    for p in range(lags[-1]):
        for stage, lag in zip(stages, lags):
            if p >= lag:
                stage(p - lag, 2)

    @pl.loop(lags[-1], last)
    def _(p):
        for stage, lag in zip(stages, lags):
            stage(p - lag, 2)

    for p in range(last, last + lags[-1] + 1):
        for stage, lag in zip(stages, lags):
            if p - lag <= last:
                stage(p - lag, 2 if p - lag < last else 1)

    y = jnp.dot(fin[...].reshape(2 * PAIRS * 16, BLOCK), perm[...], preferred_element_type=F32)
    y = y[: PAIRS * 16] + y[PAIRS * 16 :]
    for t in range(TILES):
        lanes = pl.ds(t * BLOCK, BLOCK)
        out[:, lanes] = (
            res_v[:, lanes].astype(F32) + y[8 * t : 8 * t + 8] * scl_v[:, lanes]
        ).astype(BF16)

    for copy in sent1 + sent2:
        copy.wait_send()

    @pl.loop(0, last)
    def _(p):
        for t in range(2):
            first(p, t).wait_send()
            second(p, t).wait_send()
        for dz in (1, 2, 3):
            third(p, dz, 2).wait_send()

    first(last, 0).wait_send()
    second(last, 0).wait_send()
    for dz in (1, 2, 3):
        third(last, dz, 1).wait_send()


def shards(hidden, residual, sign_bits, packed, scales):
    width = BLOCK * TILES
    dma = pltpu.SemaphoreType.DMA
    vmem = pltpu.VMEM
    tok = TOK // GROUPS
    return pl.pallas_call(
        kernel,
        out_shape=jax.ShapeDtypeStruct((tok, width), BF16),
        in_specs=[pl.BlockSpec(memory_space=pl.ANY)] * 6,
        out_specs=pl.BlockSpec(memory_space=pltpu.VMEM),
        scratch_shapes=[
            vmem((GROUPS, tok, ROW), BF16),
            vmem((tok, width), BF16),
            vmem((1, ROW), jnp.int32),
            vmem((1, width), F32),
            vmem((ROW, ROW), BF16),
            vmem((SLOTS, LANE, ROW), F32),
            vmem((PAIRS * DIGITS, ROW, WIDE), BF16),
            vmem((BLOCK, BLOCK), BF16),
            vmem((GROUPS, tok, ROW), BF16),
            vmem((TOK, ROW), BF16),
            vmem((GROUPS, tok, ROW), BF16),
            vmem((GROUPS, tok, ROW), BF16),
            vmem((TOK, ROW), BF16),
            vmem((PAIRS, 2, NX, NZ, tok, BLOCK), BF16),
            vmem((PAIRS, 2, 2, NZ, tok, BLOCK), BF16),
            vmem((PAIRS, 2, NZ, tok, BLOCK), BF16),
            vmem((PAIRS, 2, NZ, tok, BLOCK), BF16),
            vmem((PAIRS, NZ, 2, tok, BLOCK), BF16),
            vmem((PAIRS, NZ - 1, 2, tok, BLOCK), BF16),
            vmem((2, PAIRS * 16, BLOCK), BF16),
            dma((5,)),
            dma((SLOTS,)),
            dma((GROUPS,)),
            dma((GROUPS,)),
            dma((GROUPS,)),
            dma((GROUPS,)),
            dma((PAIRS, 2)),
            dma((PAIRS, 2)),
            dma((PAIRS, 2)),
            dma((PAIRS, 2)),
            dma((PAIRS, NZ - 1)),
            dma((PAIRS, NZ - 1)),
        ],
        compiler_params=pltpu.CompilerParams(
            collective_id=0, has_side_effects=True, vmem_limit_bytes=60 * 1024 * 1024
        ),
        cost_estimate=pl.CostEstimate(flops=4_300_000_000, bytes_accessed=17_000_000, transcendentals=0),
    )(
        hidden.reshape(GROUPS, tok, ROW),
        residual,
        sign_bits.reshape(1, ROW),
        packed,
        scales.reshape(1, width),
        jnp.asarray(turn_table()),
    )


def solution(mesh):
    return jax.shard_map(
        shards,
        mesh=mesh,
        in_specs=(
            P("dp", "tensor"),
            P(("dp", "tensor"), None),
            P("tensor"),
            P("tensor", None),
            P(),
        ),
        out_specs=P(("dp", "tensor"), None),
        check_vma=False,
    )
```

time: 427 us -> 66.7 us (0.16)
  waiting for transfers between devices: 184 us -> 0 us
  local copies, waits for them, and re-layouts: 113 us -> 4.27 us
  other arithmetic: 84 us -> 0 us
  Pallas kernels: 0 us -> 62.2 us
  matrix products: 17.9 us -> 0 us
  between operations: 14.2 us -> 0.01 us
  starting transfers between devices: 9.94 us -> 0 us
    unnamed x2 -> x0, waiting for transfers between devices: 166 us -> none
    pallas_call x0 -> x1, Pallas kernels: none -> 62.2 us  [shards(): pl.pallas_call(kernel, out_shape=jax.ShapeDtypeStruct((tok, width), BF16)...]
    unnamed x4 -> x0, other arithmetic: 62.1 us -> none
    another operation x1 -> x0, local copies, waits for them, and re-layouts: 58.4 us -> none  [shards(): jnp.stack(digits, axis=2).reshape(packed.shape[0], packed.shape[1] * 5)]
    convert_element_type x3 -> x0, local copies, waits for them, and re-layouts: 44.9 us -> none  [the longest x1 44 us: shards(): jnp.stack(digits, axis=2).reshape(packed.shape[0], packed.shape[1] * 5)]
    ppermute x4 -> x0, waiting for transfers between devices: 18.1 us -> none  [partner_2(): lax.ppermute(value, axis, [(i, i ^ 1 << apart) for i in range(lax.axis_si...]
    dot_general x3 -> x0, matrix products: 17.9 us -> none  [the longest x1 14.5 us: shards(): jnp.dot(rotated, weight_codes, preferred_element_type=jnp.float32)]
    another operation x1 -> x0, other arithmetic: 16.8 us -> none  [shards(): jnp.stack(digits, axis=2).reshape(packed.shape[0], packed.shape[1] * 5)]
  transfers between devices with their start and end apart: 5 -> 0, of which waited for: 2 -> 0; matrix products, arithmetic and copies ran while one was open for 43% -> 0% of each run, Pallas kernels for 0% -> 0%
where the time goes in v1:
time: 66.7 us; the launch traced here: 66.5 us
  Pallas kernels  62.2 us (93%)
  local copies, waits for them, and re-layouts  4.27 us (6%)
    pallas_call x1, Pallas kernels, shards(): pl.pallas_call(kernel, out_shape=jax.ShapeDtypeStruct((tok, width), BF16)...  62.2 us
    unnamed x1, local copies, waits for them, and re-layouts  1.57 us
    reshape x1, local copies, waits for them, and re-layouts, shards(): scales.reshape(1, width)  1.4 us

profile of v1, /device:TPU:16, one launch (start us, length us, event | category | flops | bytes accessed | tf_op | source)
XLA Modules:
  0.0 66.5 jit_solution(3743877404230832052)
XLA Ops:
  0.0 1.3 %reshape.10.sgn = s32[1,1664]{1,0:T(1,128)} reshape(s32[1664]{0:T(1024)} %param.8) | data formatting | bytes 13312 | tf_op jit(solution)/shard_map/reshape | solution.py:341
  1.3 1.4 %reshape.11.scl = f32[1,8320]{1,0:T(1,128)} reshape(f32[8320]{0:T(1024)} %param.10) | data formatting | bytes 66560 | tf_op jit(solution)/shard_map/reshape | solution.py:343
  2.7 62.2 %shard_map.64 = bf16[8,8320]{1,0:T(8,128)(2,1)} custom-call(bf16[16,8,1664]{2,1,0:T(8,128)(2,1)} %bitcast.1, bf16[8,8320]{1,0:T(8,128)(2,1)} %res.1, s32[1,1664]{1,0:T(1,128)} %reshape.10.sgn, f32[1664,1664]{1,0:T(8,128)} %packed.1, f32[1,8320]{1,0:T(1,128)} %reshape.11.scl, bf16[1664,1664]{1,0:T(8,128)(2,1)} %constant.2.clone.turn), custom_call_target="tpu_custom_call" | custom-call | flops 4300000256 | bytes 17000000 | tf_op jit(solution)/shard_map/pallas_call | solution.py:295
  64.9 1.6 %copy.8 = bf16[8,8320]{1,0:T(8,128)(2,1)} copy(bf16[8,8320]{1,0:T(8,128)(2,1)} %shard_map.64) | data formatting | bytes 266240

commit v2 on v1

--- a/solution.py
+++ b/solution.py
@@ -83,11 +83,12 @@
 
     loads[0].wait()
     loads[1].wait()
-    flips = (2 * sgn_v[...] - 1).astype(F32)
-
-    @pl.loop(0, GROUPS)
-    def _(g):
-        hid_v[g] = (hid_v[g].astype(F32) * flips).astype(BF16)
+
+    @pl.loop(0, TILES)
+    def _(c):
+        lanes = pl.ds(pl.multiple_of(c * LANE, LANE), LANE)
+        flips = (2 * sgn_v[lanes] - 1).astype(F32).reshape(1, LANE)
+        hid_v[:, :, lanes] = (hid_v[:, :, lanes].astype(F32) * flips).astype(BF16)
 
     pl.semaphore_wait(barrier, GROUPS - 1)
 
@@ -245,7 +246,7 @@
         fin[1, rows, :] = (total - high.astype(F32)).astype(BF16)
 
     stages = (multiply, halve, spread, gather)
-    lags = (0, 1, 2, 3)
+    lags = (0, 2, 4, 6)
     last = PAIRS - 1
     for p in range(lags[-1]):
         for stage, lag in zip(stages, lags):
@@ -267,7 +268,7 @@
     for t in range(TILES):
         lanes = pl.ds(t * BLOCK, BLOCK)
         out[:, lanes] = (
-            res_v[:, lanes].astype(F32) + y[8 * t : 8 * t + 8] * scl_v[:, lanes]
+            res_v[:, lanes].astype(F32) + y[8 * t : 8 * t + 8] * scl_v[lanes].reshape(1, BLOCK)
         ).astype(BF16)
 
     for copy in sent1 + sent2:
@@ -300,8 +301,8 @@
         scratch_shapes=[
             vmem((GROUPS, tok, ROW), BF16),
             vmem((tok, width), BF16),
-            vmem((1, ROW), jnp.int32),
-            vmem((1, width), F32),
+            vmem((ROW,), jnp.int32),
+            vmem((width,), F32),
             vmem((ROW, ROW), BF16),
             vmem((SLOTS, LANE, ROW), F32),
             vmem((PAIRS * DIGITS, ROW, WIDE), BF16),
@@ -338,9 +339,9 @@
     )(
         hidden.reshape(GROUPS, tok, ROW),
         residual,
-        sign_bits.reshape(1, ROW),
+        sign_bits,
         packed,
-        scales.reshape(1, width),
+        scales,
         jnp.asarray(turn_table()),
     )
 

time: 66.7 us -> 60.4 us (0.906)
  Pallas kernels: 62.2 us -> 58.7 us
  local copies, waits for them, and re-layouts: 4.27 us -> 1.57 us
    pallas_call x1, Pallas kernels: 62.2 us -> 58.7 us  [shards(): pl.pallas_call(kernel, out_shape=jax.ShapeDtypeStruct((tok, width), BF16)...]
    reshape x2 -> x0, local copies, waits for them, and re-layouts: 2.7 us -> none  [the longest x1 1.4 us: shards(): scales.reshape(1, width)]
where the time goes in v2:
time: 60.4 us; the launch traced here: 60.3 us
  Pallas kernels  58.7 us (97%)
  local copies, waits for them, and re-layouts  1.57 us (3%)
    pallas_call x1, Pallas kernels, shards(): pl.pallas_call(kernel, out_shape=jax.ShapeDtypeStruct((tok, width), BF16)...  58.7 us
    unnamed x1, local copies, waits for them, and re-layouts  1.57 us

profile of v2, /device:TPU:16, one launch (start us, length us, event | category | flops | bytes accessed | tf_op | source)
XLA Modules:
  0.0 60.3 jit_solution(11005569533940785782)
XLA Ops:
  0.0 58.7 %shard_map.64 = bf16[8,8320]{1,0:T(8,128)(2,1)} custom-call(bf16[16,8,1664]{2,1,0:T(8,128)(2,1)} %bitcast.1, bf16[8,8320]{1,0:T(8,128)(2,1)} %res.1, s32[1664]{0:T(1024)} %sgn.1, f32[1664,1664]{1,0:T(8,128)} %packed.1, f32[8320]{0:T(1024)} %scl.1, bf16[1664,1664]{1,0:T(8,128)(2,1)} %constant.2.clone.turn), custom_call_target="tpu_custom_call" | custom-call | flops 4300000256 | bytes 17000000 | tf_op jit(solution)/shard_map/pallas_call | solution.py:296
  58.7 1.6 %copy.8 = bf16[8,8320]{1,0:T(8,128)(2,1)} copy(bf16[8,8320]{1,0:T(8,128)(2,1)} %shard_map.64) | data formatting | bytes 266240

commit v3 on v2

v3 whole, which is shorter than its diff:
```python
import math

import jax
import jax.numpy as jnp
import numpy as np
from jax import lax
from jax.experimental import pallas as pl
from jax.experimental.pallas import tpu as pltpu
from jax.sharding import PartitionSpec as P

WALSH = 2048
ODD = 13
GROUPS = 16
NX = 4
NZ = 4
TOK = 128
ROW = 1664
DIGITS = 5
LANE = 128
SUB = 8
WIDE = 2 * LANE
PAIRS = 7
TILES = 13
BLOCK = DIGITS * LANE
SLOTS = 4
HALVES = 2
NZS = NZ // HALVES
HALF_TOK = TOK // HALVES
QUADS = 4
START = (0, 7 * LANE)
WIDTH = (7 * LANE, 6 * LANE)
LAGS = (0, 2, 4, 7)
MESH = pl.DeviceIdType.MESH
F32 = jnp.float32
BF16 = jnp.bfloat16


def turn_table():
    local = ROW // ODD
    ids = np.arange(local)
    both = ids[:, None] & ids[None, :]
    parity = np.zeros_like(both)
    for bit in range(local.bit_length() - 1):
        parity ^= (both >> bit) & 1
    walsh = 1.0 - 2.0 * parity
    k = np.arange(ODD)[:, None]
    b = np.arange(ODD)[None, :]
    cosine = np.where(k == 0, math.sqrt(0.5), 1.0) * math.sqrt(2.0 / ODD)
    cosine = cosine * np.cos(math.pi * (2.0 * b + 1.0) * k / (2.0 * ODD))
    return (np.kron(walsh, cosine.T) / math.sqrt(WALSH)).astype(jnp.bfloat16)


OFFSETS = [(dz, dx) for dz in (2, 1, 3, 0) for dx in (2, 1, 3, 0) if dz or dx]


def kernel(
    hid, res, sgn, packed, scl, turn, out,
    hid_v, res_v, sgn_v, scl_v, turn_v, words, codes, perm,
    rx, tx, rr, mixed, lhs, part, in1, out2, in2, summed, in3, fin,
    load_sem, word_sem, s1, r1, s2, r2, sx1, rx1, sx2, rx2, sz, rz,
):
    me = lax.axis_index("tensor")
    z, x = me // NX, me % NX
    loads = []
    for n, (src, dst) in enumerate(
        ((hid, hid_v), (sgn, sgn_v), (turn, turn_v), (res, res_v), (scl, scl_v))
    ):
        loads.append(pltpu.make_async_copy(src, dst, load_sem.at[n]))

    def word_copy(r, slot):
        return pltpu.make_async_copy(
            packed.at[pl.ds(pl.multiple_of(r * LANE, LANE), LANE)], words.at[slot], word_sem.at[slot]
        )

    loads[0].start()
    loads[1].start()
    barrier = pltpu.get_barrier_semaphore()
    for dz, dx in OFFSETS:
        peer = (z + dz) % NZ * NX + (x + dx) % NX
        pl.semaphore_signal(barrier, inc=1, device_id={"tensor": peer}, device_id_type=MESH)
    for r in range(SLOTS):
        word_copy(r, r).start()
    for n in (2, 3, 4):
        loads[n].start()

    loads[0].wait()
    loads[1].wait()

    @pl.loop(0, TILES)
    def _(c):
        lanes = pl.ds(pl.multiple_of(c * LANE, LANE), LANE)
        flips = (2 * sgn_v[lanes] - 1).astype(F32).reshape(1, LANE)
        hid_v[:, :, lanes] = (hid_v[:, :, lanes].astype(F32) * flips).astype(BF16)

    def by_parity(run):
        for parity in range(2):

            @pl.when(x % 2 == parity)
            def _():
                run(parity)

    def z_of(h, n):
        return 3 * n if h == 0 else 1 + n

    def in_half(h):
        return (z % 3 == 0) if h == 0 else (z % 3 != 0)

    def place_in_half(h):
        return z // 3 if h == 0 else z - 1

    def group(h, number):
        return z_of(h, number // 2 // NX) * NX + number // 2 % NX

    def scatter(h, dz, dx, parity):
        peer = (z + dz) % NZ * NX + (x + dx) % NX
        theirs = (parity + dx) % 2
        off = dz * NX + dx
        return pltpu.make_async_remote_copy(
            src_ref=hid_v.at[group(h, peer), :, pl.ds(START[theirs], WIDTH[theirs])],
            dst_ref=rx.at[h, me, :, pl.ds(0, WIDTH[theirs])],
            send_sem=s1.at[h, off], recv_sem=r1.at[h, off],
            device_id={"tensor": peer}, device_id_type=MESH,
        )

    def scattered(h, dz, dx, parity):
        source = (z + NZ - dz) % NZ * NX + (x + NX - dx) % NX
        off = dz * NX + dx
        there = rx.at[h, source, :, pl.ds(0, WIDTH[parity])]
        return pltpu.make_async_remote_copy(
            src_ref=there, dst_ref=there, send_sem=s1.at[h, off], recv_sem=r1.at[h, off],
            device_id={"tensor": source}, device_id_type=MESH,
        )

    def back(h, dz, dx, parity):
        peer = (z + dz) % NZ * NX + (x + dx) % NX
        off = dz * NX + dx
        return pltpu.make_async_remote_copy(
            src_ref=tx.at[h, peer, :, pl.ds(0, WIDTH[parity])],
            dst_ref=rr.at[h, me // 2, :, pl.ds(START[parity], WIDTH[parity])],
            send_sem=s2.at[h, off], recv_sem=r2.at[h, off],
            device_id={"tensor": peer}, device_id_type=MESH,
        )

    def came_back(h, dz, dx, parity):
        source = (z + NZ - dz) % NZ * NX + (x + NX - dx) % NX
        theirs = (parity + dx) % 2
        off = dz * NX + dx
        there = rr.at[h, source // 2, :, pl.ds(START[theirs], WIDTH[theirs])]
        return pltpu.make_async_remote_copy(
            src_ref=there, dst_ref=there, send_sem=s2.at[h, off], recv_sem=r2.at[h, off],
            device_id={"tensor": source}, device_id_type=MESH,
        )

    def send_out(h):
        def run(parity):
            for dz, dx in OFFSETS:
                scatter(h, dz, dx, parity).start()
            rx[h, me, :, : WIDTH[parity]] = hid_v[
                group(h, me), :, START[parity] : START[parity] + WIDTH[parity]
            ]

        by_parity(run)

    def mix(h):
        def wait(parity):
            for dz, dx in OFFSETS:
                scattered(h, dz, dx, parity).wait_recv()

        by_parity(wait)

        def mix_tile(c):
            lanes = pl.ds(c * LANE, LANE)
            blocks = [rx[h, g, :, lanes].astype(F32) for g in range(GROUPS)]
            span = 1
            while span < GROUPS:
                for g in range(GROUPS):
                    if not g & span:
                        a, b = blocks[g], blocks[g + span]
                        blocks[g], blocks[g + span] = a + b, a - b
                span *= 2
            for g in range(GROUPS):
                tx[h, g, :, lanes] = blocks[g].astype(BF16)

        for c in range(6):
            mix_tile(c)

        @pl.when(x % 2 == 0)
        def _():
            mix_tile(6)

        def run(parity):
            for dz, dx in OFFSETS:
                back(h, dz, dx, parity).start()
            rr[h, me // 2, :, START[parity] : START[parity] + WIDTH[parity]] = tx[h, me, :, : WIDTH[parity]]

        by_parity(run)

    def local_turn(h):
        def wait(parity):
            for dz, dx in OFFSETS:
                came_back(h, dz, dx, parity).wait_recv()

        by_parity(wait)

        for c in range(TILES):
            lanes = pl.ds(c * LANE, LANE)
            mixed[:, lanes] = rr[h, :, :, lanes].astype(F32).reshape(HALF_TOK, LANE).astype(BF16)

        def turned(start, wide):
            lanes = pl.ds(start, wide)
            y = jnp.dot(mixed[...], turn_v[:, lanes], preferred_element_type=F32)
            lhs[h, :, lanes] = y.astype(BF16)

        for c in range(PAIRS - 1):
            turned(c * WIDE, WIDE)

        turned((PAIRS - 1) * WIDE, LANE)

    def unpack(r):
        slot = r % SLOTS
        word_copy(r, slot).wait()
        rows = pl.ds(pl.multiple_of(r * LANE, LANE), LANE)
        for p in range(PAIRS):
            wide = WIDE if p < PAIRS - 1 else LANE
            word = words[slot, :, p * WIDE : p * WIDE + wide].astype(jnp.int32) ^ 0x88888
            for k in range(DIGITS):
                digit = (word << (28 - 4 * k)) >> 28
                codes[p * DIGITS + k, rows, :wide] = digit.astype(F32).astype(BF16)

        @pl.when(r + SLOTS < TILES)
        def _():
            word_copy(r + SLOTS, slot).start()

    pl.semaphore_wait(barrier, GROUPS - 1)
    send_out(0)
    stops = (0, 5, 9, TILES)

    @pl.loop(stops[0], stops[1])
    def _(r):
        unpack(r)

    mix(0)

    @pl.loop(stops[1], stops[2])
    def _(r):
        unpack(r)


    @pl.loop(stops[2], stops[3])
    def _(r):
        unpack(r)

    rows = lax.broadcasted_iota(jnp.int32, (BLOCK, BLOCK), 0)
    cols = lax.broadcasted_iota(jnp.int32, (BLOCK, BLOCK), 1)
    perm[...] = jnp.where((rows & (LANE - 1)) * DIGITS + (rows >> 7) == cols, 1.0, 0.0).astype(BF16)
    fin[...] = jnp.zeros_like(fin)
    for n in (2, 3, 4):
        loads[n].wait()

    across = (x + 1 - 2 * (x % 2), 3 - x)
    half = ((x + 1) // 2 % 2, x // 2)
    mine = (x // 2, x % 2)
    place = ((0, 2, 3, 1), (0, 1, 2, 3))

    def shape(h, c):
        return ((0, 1), 2) if c < QUADS - 1 else ((h,), 1)

    def first(h, c, t, pairs):
        return pltpu.make_async_remote_copy(
            src_ref=part.at[h, c, t, pl.ds(2 * (1 - half[t]), 2), pl.ds(0, pairs)],
            dst_ref=in1.at[h, c, t, :, pl.ds(0, pairs)],
            send_sem=sx1.at[h, c, t], recv_sem=rx1.at[h, c, t],
            device_id={"tensor": z * NX + across[t]}, device_id_type=MESH,
        )

    def second(h, c, t, pairs):
        return pltpu.make_async_remote_copy(
            src_ref=out2.at[h, c, t, pl.ds(0, pairs)], dst_ref=in2.at[h, c, t, pl.ds(0, pairs)],
            send_sem=sx2.at[h, c, t], recv_sem=rx2.at[h, c, t],
            device_id={"tensor": z * NX + across[1 - t]}, device_id_type=MESH,
        )

    def third(h, c, n):
        kinds, pairs = shape(h, c)
        there = z_of(h, n)
        off = (there + NZ - z) % NZ
        which = (pl.ds(kinds[0], len(kinds)), pl.ds(0, pairs))
        return off, pltpu.make_async_remote_copy(
            src_ref=summed.at[h, c, n, *which], dst_ref=in3.at[h, c, (off + NZ - 1) % NZ, *which],
            send_sem=sz.at[h, c, n], recv_sem=rz.at[h, c, (off + NZ - 1) % NZ],
            device_id={"tensor": there * NX + x}, device_id_type=MESH,
        )

    def third_in(h, c, off):
        kinds, pairs = shape(h, c)
        which = (pl.ds(kinds[0], len(kinds)), pl.ds(0, pairs))
        there = in3.at[h, c, off - 1, *which]
        return pltpu.make_async_remote_copy(
            src_ref=there, dst_ref=there, send_sem=sz.at[h, c, 0], recv_sem=rz.at[h, c, off - 1],
            device_id={"tensor": (z + NZ - off) % NZ * NX + x}, device_id_type=MESH,
        )

    def multiply(h, c):
        kinds, pairs = shape(h, c)

        for k in range(DIGITS):
            lanes = pl.ds(k * LANE, LANE)
            for n in range(pairs):
                wide = LANE * len(kinds)
                code = codes[(2 * c + n) * DIGITS + k, :, :wide]
                y = jnp.dot(lhs[h], code, preferred_element_type=F32)
                y = y.reshape(NZS, NX, SUB, wide)
                for i, t in enumerate(kinds):
                    for xx in range(NX):
                        part[h, c, t, place[t][xx], n, :, :, lanes] = y[
                            :, xx, :, i * LANE : (i + 1) * LANE
                        ].astype(BF16)

        for t in kinds:
            first(h, c, t, pairs).start()

    def halve(h, c):
        kinds, pairs = shape(h, c)
        for t in kinds:
            first(h, c, t, pairs).wait_recv()
            other = 1 - mine[t]
            total = part[h, c, t, 2 * half[t] + other, :pairs].astype(F32)
            out2[h, c, t, :pairs] = (total + in1[h, c, t, other, :pairs].astype(F32)).astype(BF16)
            second(h, c, t, pairs).start()

    def spread(h, c):
        kinds, pairs = shape(h, c)
        for t in kinds:
            second(h, c, t, pairs).wait_recv()
            total = part[h, c, t, 2 * half[t] + mine[t], :pairs].astype(F32)
            total = total + in1[h, c, t, mine[t], :pairs].astype(F32)
            total = (total + in2[h, c, t, :pairs].astype(F32)).astype(BF16)
            for n in range(NZS):
                summed[h, c, n, t, :pairs] = total[:, n]
        for n in range(NZS):
            off, copy = third(h, c, n)

            @pl.when(off != 0)
            def _():
                copy.start()

    def gather(h, c):
        kinds, pairs = shape(h, c)
        n = place_in_half(h)

        @pl.when(in_half(h))
        def _():
            for off in range(1, NZ):
                third_in(h, c, off).wait_recv()
            for q in range(pairs):
                totals = []
                for t in kinds:
                    total = summed[h, c, n, t, q].astype(F32)
                    for m in range(NZ - 1):
                        total = total + in3[h, c, m, t, q].astype(F32)
                    totals.append(total)
                if len(totals) == 1:
                    totals.append(jnp.zeros_like(totals[0]))
                total = jnp.concatenate(totals, axis=0)
                high = total.astype(BF16)
                rows = pl.ds((2 * c + q) * 16, 16)
                fin[0, rows, :] = high
                fin[1, rows, :] = (total - high.astype(F32)).astype(BF16)

    last = QUADS - 1
    chunks = [(0, last)] + [(0, c) for c in range(last)] + [(1, c) for c in range(QUADS)]
    stages = (multiply, halve, spread, gather)
    for step in range(len(chunks) + LAGS[-1]):
        if step < len(chunks) and (step == 0 or chunks[step][0] != chunks[step - 1][0]):
            local_turn(chunks[step][0])
            if step == 0:
                send_out(1)
        if step == 3:
            mix(1)
        for stage, lag in zip(stages, LAGS):
            if 0 <= step - lag < len(chunks):
                stage(*chunks[step - lag])

    y = jnp.dot(fin[...].reshape(2 * PAIRS * 16, BLOCK), perm[...], preferred_element_type=F32)
    y = y[: PAIRS * 16] + y[PAIRS * 16 :]
    for t in range(TILES):
        lanes = pl.ds(t * BLOCK, BLOCK)
        out[:, lanes] = (
            res_v[:, lanes].astype(F32) + y[8 * t : 8 * t + 8] * scl_v[lanes].reshape(1, BLOCK)
        ).astype(BF16)

    def drain(parity):
        for h in range(HALVES):
            for dz, dx in OFFSETS:
                scatter(h, dz, dx, parity).wait_send()
                back(h, dz, dx, parity).wait_send()

    by_parity(drain)
    for h, c in chunks:
        kinds, pairs = shape(h, c)
        for t in kinds:
            first(h, c, t, pairs).wait_send()
            second(h, c, t, pairs).wait_send()
        for n in range(NZS):
            off, copy = third(h, c, n)

            @pl.when(off != 0)
            def _():
                copy.wait_send()


def shards(hidden, residual, sign_bits, packed, scales):
    width = BLOCK * TILES
    dma = pltpu.SemaphoreType.DMA
    vmem = pltpu.VMEM
    tok = TOK // GROUPS
    return pl.pallas_call(
        kernel,
        out_shape=jax.ShapeDtypeStruct((tok, width), BF16),
        in_specs=[pl.BlockSpec(memory_space=pl.ANY)] * 6,
        out_specs=pl.BlockSpec(memory_space=pltpu.VMEM),
        scratch_shapes=[
            vmem((GROUPS, tok, ROW), BF16),
            vmem((tok, width), BF16),
            vmem((ROW,), jnp.int32),
            vmem((width,), F32),
            vmem((ROW, ROW), BF16),
            vmem((SLOTS, LANE, ROW), F32),
            vmem((PAIRS * DIGITS, ROW, WIDE), BF16),
            vmem((BLOCK, BLOCK), BF16),
            vmem((HALVES, GROUPS, tok, WIDTH[0]), BF16),
            vmem((HALVES, GROUPS, tok, WIDTH[0]), BF16),
            vmem((HALVES, GROUPS // 2, tok, ROW), BF16),
            vmem((HALF_TOK, ROW), BF16),
            vmem((HALVES, HALF_TOK, ROW), BF16),
            vmem((HALVES, QUADS, 2, NX, 2, NZS, tok, BLOCK), BF16),
            vmem((HALVES, QUADS, 2, 2, 2, NZS, tok, BLOCK), BF16),
            vmem((HALVES, QUADS, 2, 2, NZS, tok, BLOCK), BF16),
            vmem((HALVES, QUADS, 2, 2, NZS, tok, BLOCK), BF16),
            vmem((HALVES, QUADS, NZS, 2, 2, tok, BLOCK), BF16),
            vmem((HALVES, QUADS, NZ - 1, 2, 2, tok, BLOCK), BF16),
            vmem((2, PAIRS * 16, BLOCK), BF16),
            dma((5,)),
            dma((SLOTS,)),
            dma((HALVES, GROUPS)),
            dma((HALVES, GROUPS)),
            dma((HALVES, GROUPS)),
            dma((HALVES, GROUPS)),
            dma((HALVES, QUADS, 2)),
            dma((HALVES, QUADS, 2)),
            dma((HALVES, QUADS, 2)),
            dma((HALVES, QUADS, 2)),
            dma((HALVES, QUADS, NZS)),
            dma((HALVES, QUADS, NZ - 1)),
        ],
        compiler_params=pltpu.CompilerParams(
            collective_id=0, has_side_effects=True, vmem_limit_bytes=60 * 1024 * 1024
        ),
        cost_estimate=pl.CostEstimate(flops=4_300_000_000, bytes_accessed=17_000_000, transcendentals=0),
    )(
        hidden.reshape(GROUPS, tok, ROW),
        residual,
        sign_bits,
        packed,
        scales,
        jnp.asarray(turn_table()),
    )


def solution(mesh):
    return jax.shard_map(
        shards,
        mesh=mesh,
        in_specs=(
            P("dp", "tensor"),
            P(("dp", "tensor"), None),
            P("tensor"),
            P("tensor", None),
            P(),
        ),
        out_specs=P(("dp", "tensor"), None),
        check_vma=False,
    )
```

time: 60.4 us -> 55 us (0.911)
  the two profiles are of different devices: /device:TPU:16 before, /device:TPU:32 now
where the time goes in v3:
time: 55 us; the launch traced here: 54.9 us
  Pallas kernels  53.3 us (97%)
  local copies, waits for them, and re-layouts  1.57 us (3%)
    pallas_call x1, Pallas kernels, shards(): pl.pallas_call(kernel, out_shape=jax.ShapeDtypeStruct((tok, width), BF16)...  53.3 us
    unnamed x1, local copies, waits for them, and re-layouts  1.57 us

profile of v3, /device:TPU:32, one launch (start us, length us, event | category | flops | bytes accessed | tf_op | source)
XLA Modules:
  0.0 54.9 jit_solution(9846337909391663986)
XLA Ops:
  0.0 53.3 %shard_map.64 = bf16[8,8320]{1,0:T(8,128)(2,1)} custom-call(bf16[16,8,1664]{2,1,0:T(8,128)(2,1)} %bitcast.1, bf16[8,8320]{1,0:T(8,128)(2,1)} %res.1, s32[1664]{0:T(1024)} %sgn.1, f32[1664,1664]{1,0:T(8,128)} %packed.1, f32[8320]{0:T(1024)} %scl.1, bf16[1664,1664]{1,0:T(8,128)(2,1)} %constant.2.clone.turn), custom_call_target="tpu_custom_call" | custom-call | flops 4300000256 | bytes 17000000 | tf_op jit(solution)/shard_map/pallas_call | solution.py:417
  53.3 1.6 %copy.8 = bf16[8,8320]{1,0:T(8,128)(2,1)} copy(bf16[8,8320]{1,0:T(8,128)(2,1)} %shard_map.64) | data formatting | bytes 266240

commit v4 on v3

--- a/solution.py
+++ b/solution.py
@@ -201,6 +201,8 @@
                 came_back(h, dz, dx, parity).wait_recv()
 
         by_parity(wait)
+        if h == 0:
+            send_out(1)
 
         for c in range(TILES):
             lanes = pl.ds(c * LANE, LANE)
@@ -373,9 +375,7 @@
     for step in range(len(chunks) + LAGS[-1]):
         if step < len(chunks) and (step == 0 or chunks[step][0] != chunks[step - 1][0]):
             local_turn(chunks[step][0])
-            if step == 0:
-                send_out(1)
-        if step == 3:
+        if step == 2:
             mix(1)
         for stage, lag in zip(stages, LAGS):
             if 0 <= step - lag < len(chunks):

time: 55 us -> 54.3 us (0.987)
  the two profiles are of different devices: /device:TPU:32 before, /device:TPU:56 now
where the time goes in v4:
time: 54.3 us; the launch traced here: 54.2 us
  Pallas kernels  52.6 us (97%)
  local copies, waits for them, and re-layouts  1.57 us (3%)
    pallas_call x1, Pallas kernels, shards(): pl.pallas_call(kernel, out_shape=jax.ShapeDtypeStruct((tok, width), BF16)...  52.6 us
    unnamed x1, local copies, waits for them, and re-layouts  1.57 us

profile of v4, /device:TPU:56, one launch (start us, length us, event | category | flops | bytes accessed | tf_op | source)
XLA Modules:
  0.0 54.2 jit_solution(16248480947524353723)
XLA Ops:
  0.0 52.6 %shard_map.64 = bf16[8,8320]{1,0:T(8,128)(2,1)} custom-call(bf16[16,8,1664]{2,1,0:T(8,128)(2,1)} %bitcast.1, bf16[8,8320]{1,0:T(8,128)(2,1)} %res.1, s32[1664]{0:T(1024)} %sgn.1, f32[1664,1664]{1,0:T(8,128)} %packed.1, f32[8320]{0:T(1024)} %scl.1, bf16[1664,1664]{1,0:T(8,128)(2,1)} %constant.2.clone.turn), custom_call_target="tpu_custom_call" | custom-call | flops 4300000256 | bytes 17000000 | tf_op jit(solution)/shard_map/pallas_call | solution.py:417
  52.6 1.6 %copy.8 = bf16[8,8320]{1,0:T(8,128)(2,1)} copy(bf16[8,8320]{1,0:T(8,128)(2,1)} %shard_map.64) | data formatting | bytes 266240
